TPU v7x, 32 devices: a whole 2x2x4 slice. The times are simulated.
32 devices in a mesh: pitch: 8 (over z, x), span: 4 (over y, core).
Axes of the slice: x: 2, y: 2, z: 4, core: 2. Of those that a mesh axis runs over, the one named last changes fastest.
Arguments:
- adjoint: float32 [5, 32, 64, 256], P(None, 'pitch', 'span'), may hold values from -6 to 6
- gradient: float32 [5, 32, 64, 256], P(None, 'pitch', 'span'), may hold values from -6 to 6
- diag_blocks: bfloat16 [5, 5, 32, 64, 256], P(None, None, 'pitch', 'span')
- off_blocks: bfloat16 [6, 5, 5, 32, 64, 256], P(None, None, None, 'pitch', 'span'), may hold values from -2.5 to 2.5
- precond: bfloat16 [5, 5, 32, 64, 256], P(None, None, 'pitch', 'span')
- low_donor: int32 [64, 256, 2], P('span'), may hold values from 0 to 4095
- low_weight: float32 [64, 256, 2], P('span'), may hold values from 0.2 to 1
- high_donor: int32 [64, 256, 2], P('span'), may hold values from 0 to 4095
- high_weight: float32 [64, 256, 2], P('span'), may hold values from 0.2 to 1
- tip_mask: int32 [32, 64, 256], P('pitch', 'span'), may hold values 0 or 1
Outputs:
- adjoint_out: float32 [5, 32, 64, 256], P(None, 'pitch', 'span')
Inputs may be any that keep to these rules, and one draw needn't show every extreme that they name: `low_donor`: each id names a cell of the opposite pitch end within the span rows of the receiving cell's span block of 16 rows. `high_donor`: each id names a cell of the opposite pitch end within the span rows of the receiving cell's span block of 16 rows.
All inputs are finite; a program needn't handle non-finite values. No bound on the sum of `tip_mask` on one device may be relied on, other than what follows from the above.
Results may differ from a plain program's by a relative error of at most 0.0003.
Values sent between devices are 32-bit elements; how exact they have to be, the bound alone decides.
A program may use at most 64 MiB of HBM per device.

v0:
```python
import math

import jax
import jax.numpy as jnp
from jax import lax
from jax.sharding import PartitionSpec as P

ITERS = 2


def extended(shard, sides, width):
    for axis, dim in sides:
        size, length = (lax.axis_size(axis), shard.shape[dim])
        up = [(i, (i + 1) % size) for i in range(size - 1)]
        down = [(j, i) for i, j in up]
        last = lax.slice_in_dim(shard, length - width, length, axis=dim)
        first = lax.slice_in_dim(shard, 0, width, axis=dim)
        before = lax.ppermute(last, axis, up)
        after = lax.ppermute(first, axis, down)
        shard = jnp.concatenate([before, shard, after], axis=dim)
    return shard


def passed_along(shard, axis, by):
    size = lax.axis_size(axis)
    return lax.ppermute(shard, axis, [(i, (i + by) % size) for i in range(size)])


def shift_forward(field, axis):
    widths = [(0, 0)] * field.ndim
    widths[axis] = (1, 0)
    return lax.slice_in_dim(jnp.pad(field, widths), 0, field.shape[axis], axis=axis)


def shift_backward(field, axis):
    widths = [(0, 0)] * field.ndim
    widths[axis] = (0, 1)
    return lax.slice_in_dim(jnp.pad(field, widths), 1, field.shape[axis] + 1, axis=axis)


def scatter_face(values, donors, weights):
    planes = values.shape[0]
    cells = donors.shape[0] * donors.shape[1]
    entries = donors.shape[2]
    flat_values = values.reshape(planes, cells)
    flat_donors = donors.reshape(cells, entries)
    flat_weights = weights.reshape(cells, entries)
    width = math.gcd(cells, 512)
    blocks = cells // width

    def one_block(start):
        targets = start + lax.iota(jnp.int32, width)
        matrix = jnp.zeros((width, cells), jnp.float32)
        for entry in range(entries):
            hits = flat_donors[:, entry][None, :] == targets[:, None]
            matrix = matrix + jnp.where(hits, flat_weights[:, entry][None, :], 0.0)
        return jnp.einsum("ps,ts->pt", flat_values, matrix, precision=lax.Precision.HIGHEST)

    starts = lax.iota(jnp.int32, blocks) * width
    pieces = lax.map(one_block, starts)
    return jnp.transpose(pieces, (1, 0, 2)).reshape(values.shape)


def body(
    adjoint,
    gradient,
    diag_blocks,
    off_blocks,
    precond,
    low_donor,
    low_weight,
    high_donor,
    high_weight,
    tip_mask,
):
    highest = lax.Precision.HIGHEST
    pitch_index = lax.axis_index("pitch")
    pitch_count = lax.axis_size("pitch")
    local_pitch = adjoint.shape[1]
    local_span = adjoint.shape[2]
    step_size = jnp.where(tip_mask == 1, 0.3, 0.6).astype(jnp.float32)
    is_first = pitch_index == 0
    is_last = pitch_index == pitch_count - 1
    for sweep in range(ITERS):
        outgoing = jnp.einsum(
            "dabpsx,apsx->dbpsx", off_blocks.astype(jnp.float32), adjoint, precision=highest
        )
        applied = jnp.einsum(
            "abpsx,apsx->bpsx", diag_blocks.astype(jnp.float32), adjoint, precision=highest
        )
        applied = applied + shift_backward(outgoing[0], 1) + shift_forward(outgoing[1], 1)
        applied = applied + shift_backward(outgoing[4], 3) + shift_forward(outgoing[5], 3)
        span_terms = jnp.stack([outgoing[2], outgoing[3]])
        padded = extended(span_terms, (("span", 3),), 1)
        applied = applied + padded[0, :, :, 2 : local_span + 2] + padded[1, :, :, 0:local_span]
        low_face = outgoing[0][:, 0]
        high_face = outgoing[1][:, local_pitch - 1]
        to_high = scatter_face(low_face, low_donor, low_weight)
        to_low = scatter_face(high_face, high_donor, high_weight)
        upward = jnp.where(is_last, to_low, high_face)
        downward = jnp.where(is_first, to_high, low_face)
        from_below = passed_along(upward, "pitch", 1)
        from_above = passed_along(downward, "pitch", -1)
        applied = applied.at[:, 0].add(from_below)
        applied = applied.at[:, local_pitch - 1].add(from_above)
        update = jnp.einsum(
            "abpsx,bpsx->apsx", precond.astype(jnp.float32), applied + gradient, precision=highest
        )
        adjoint = adjoint - step_size[None] * update
    return adjoint


def solution(mesh):
    return jax.shard_map(
        body,
        mesh=mesh,
        in_specs=(
            P(None, "pitch", "span", None),
            P(None, "pitch", "span", None),
            P(None, None, "pitch", "span", None),
            P(None, None, None, "pitch", "span", None),
            P(None, None, "pitch", "span", None),
            P("span", None, None),
            P("span", None, None),
            P("span", None, None),
            P("span", None, None),
            P("pitch", "span", None),
        ),
        out_specs=P(None, "pitch", "span", None),
        check_vma=False,
    )
```

profile of v0, /device:TPU:0, one launch (start us, length us, event | category | flops | bytes accessed | tf_op | source)
XLA Modules:
  0.0 366.8 jit_solution(11633837011264725464)
XLA Ops:
  0.0 3.8 %fusion.76 = f32[4,16,256,6,5]{2,1,0,4,3:T(8,128)S(1)} fusion(f32[4,16,256,5]{2,1,0,3:T(8,128)} %bitcast.229, bf16[6,5,5,4,16,256]{5,4,3,2,1,0:T(8,128)(2,1)} %param.29), kind=kLoop, calls=%fused_computation.66 | loop fusion | flops 6881280 | bytes 7208960
  4.0 0.7 fusion.112
  4.7 3.0 collective-permute-start.1
  7.7 1.3 collective-permute-start
  9.0 1.0 slice_bitcast_fusion.4
  10.1 76.8 %while.44 = (s32[]{:T(128)}, f32[8,5,512]{2,1,0:T(8,128)S(1)}, s32[4096,2]{0,1:T(2,128)S(1)}, s32[8]{0:T(128)S(1)}, f32[4096,2]{0,1:T(2,128)S(1)}, /*index=5*/f32[5,4096]{1,0:T(8,128)S(1)}, s32[]{:T(128)}) while((s32[]{:T(128)}, f32[8,5,512]{2,1,0:T(8,128)S(1)}, s32[4096,2]{0,1:T(2,128)S(1)}, s32[8]{0:T(128)S(1)}, f32[4096,2]{0,1:T(2,128)S(1)}, ...), condition=%wide.region_1.2_spmd, body=%wide.region_0.1_spmd.sunk | while | flops 136315392 | bytes 348265 | solution.py:60
  11.3 8.4 %fusion.143 = f32[8,5,512]{2,1,0:T(8,128)S(1)} fusion(f32[8,5,512]{2,1,0:T(8,128)S(1)} %get-tuple-element.449, s32[]{:T(128)S(6)} %copy.100, f32[5,4096]{1,0:T(8,128)S(1)} %get-tuple-element.460, f32[4096]{0:T(1024)S(1)} %bitcast.240, s32[4096]{0:T(1024)S(1)} %bitcast.248, f32[4096]{0:T(1024)S(1)} %bitcast.239, s32[4096]{0:T(1024)S(1)} %bitcast.247, ...), kind=kOutput, calls=%fused_computation.13.clone.1 | convolution fusion | flops 136314880 | bytes 215044 | tf_op jit(solution)/shard_map/while/body/eval_jaxpr/ps,ts->pt/dot_general | solution.py:57
  20.9 8.4 %fusion.143 = f32[8,5,512]{2,1,0:T(8,128)S(1)} fusion(f32[8,5,512]{2,1,0:T(8,128)S(1)} %get-tuple-element.449, s32[]{:T(128)S(6)} %copy.100, f32[5,4096]{1,0:T(8,128)S(1)} %get-tuple-element.460, f32[4096]{0:T(1024)S(1)} %bitcast.240, s32[4096]{0:T(1024)S(1)} %bitcast.248, f32[4096]{0:T(1024)S(1)} %bitcast.239, s32[4096]{0:T(1024)S(1)} %bitcast.247, ...), kind=kOutput, calls=%fused_computation.13.clone.1 | convolution fusion | flops 136314880 | bytes 215044 | tf_op jit(solution)/shard_map/while/body/eval_jaxpr/ps,ts->pt/dot_general | solution.py:57
  30.5 8.4 %fusion.143 = f32[8,5,512]{2,1,0:T(8,128)S(1)} fusion(f32[8,5,512]{2,1,0:T(8,128)S(1)} %get-tuple-element.449, s32[]{:T(128)S(6)} %copy.100, f32[5,4096]{1,0:T(8,128)S(1)} %get-tuple-element.460, f32[4096]{0:T(1024)S(1)} %bitcast.240, s32[4096]{0:T(1024)S(1)} %bitcast.248, f32[4096]{0:T(1024)S(1)} %bitcast.239, s32[4096]{0:T(1024)S(1)} %bitcast.247, ...), kind=kOutput, calls=%fused_computation.13.clone.1 | convolution fusion | flops 136314880 | bytes 215044 | tf_op jit(solution)/shard_map/while/body/eval_jaxpr/ps,ts->pt/dot_general | solution.py:57
  40.1 8.4 %fusion.143 = f32[8,5,512]{2,1,0:T(8,128)S(1)} fusion(f32[8,5,512]{2,1,0:T(8,128)S(1)} %get-tuple-element.449, s32[]{:T(128)S(6)} %copy.100, f32[5,4096]{1,0:T(8,128)S(1)} %get-tuple-element.460, f32[4096]{0:T(1024)S(1)} %bitcast.240, s32[4096]{0:T(1024)S(1)} %bitcast.248, f32[4096]{0:T(1024)S(1)} %bitcast.239, s32[4096]{0:T(1024)S(1)} %bitcast.247, ...), kind=kOutput, calls=%fused_computation.13.clone.1 | convolution fusion | flops 136314880 | bytes 215044 | tf_op jit(solution)/shard_map/while/body/eval_jaxpr/ps,ts->pt/dot_general | solution.py:57
  49.7 8.4 %fusion.143 = f32[8,5,512]{2,1,0:T(8,128)S(1)} fusion(f32[8,5,512]{2,1,0:T(8,128)S(1)} %get-tuple-element.449, s32[]{:T(128)S(6)} %copy.100, f32[5,4096]{1,0:T(8,128)S(1)} %get-tuple-element.460, f32[4096]{0:T(1024)S(1)} %bitcast.240, s32[4096]{0:T(1024)S(1)} %bitcast.248, f32[4096]{0:T(1024)S(1)} %bitcast.239, s32[4096]{0:T(1024)S(1)} %bitcast.247, ...), kind=kOutput, calls=%fused_computation.13.clone.1 | convolution fusion | flops 136314880 | bytes 215044 | tf_op jit(solution)/shard_map/while/body/eval_jaxpr/ps,ts->pt/dot_general | solution.py:57
  59.3 8.4 %fusion.143 = f32[8,5,512]{2,1,0:T(8,128)S(1)} fusion(f32[8,5,512]{2,1,0:T(8,128)S(1)} %get-tuple-element.449, s32[]{:T(128)S(6)} %copy.100, f32[5,4096]{1,0:T(8,128)S(1)} %get-tuple-element.460, f32[4096]{0:T(1024)S(1)} %bitcast.240, s32[4096]{0:T(1024)S(1)} %bitcast.248, f32[4096]{0:T(1024)S(1)} %bitcast.239, s32[4096]{0:T(1024)S(1)} %bitcast.247, ...), kind=kOutput, calls=%fused_computation.13.clone.1 | convolution fusion | flops 136314880 | bytes 215044 | tf_op jit(solution)/shard_map/while/body/eval_jaxpr/ps,ts->pt/dot_general | solution.py:57
  68.9 8.4 %fusion.143 = f32[8,5,512]{2,1,0:T(8,128)S(1)} fusion(f32[8,5,512]{2,1,0:T(8,128)S(1)} %get-tuple-element.449, s32[]{:T(128)S(6)} %copy.100, f32[5,4096]{1,0:T(8,128)S(1)} %get-tuple-element.460, f32[4096]{0:T(1024)S(1)} %bitcast.240, s32[4096]{0:T(1024)S(1)} %bitcast.248, f32[4096]{0:T(1024)S(1)} %bitcast.239, s32[4096]{0:T(1024)S(1)} %bitcast.247, ...), kind=kOutput, calls=%fused_computation.13.clone.1 | convolution fusion | flops 136314880 | bytes 215044 | tf_op jit(solution)/shard_map/while/body/eval_jaxpr/ps,ts->pt/dot_general | solution.py:57
  78.5 8.4 %fusion.143 = f32[8,5,512]{2,1,0:T(8,128)S(1)} fusion(f32[8,5,512]{2,1,0:T(8,128)S(1)} %get-tuple-element.449, s32[]{:T(128)S(6)} %copy.100, f32[5,4096]{1,0:T(8,128)S(1)} %get-tuple-element.460, f32[4096]{0:T(1024)S(1)} %bitcast.240, s32[4096]{0:T(1024)S(1)} %bitcast.248, f32[4096]{0:T(1024)S(1)} %bitcast.239, s32[4096]{0:T(1024)S(1)} %bitcast.247, ...), kind=kOutput, calls=%fused_computation.13.clone.1 | convolution fusion | flops 136314880 | bytes 215044 | tf_op jit(solution)/shard_map/while/body/eval_jaxpr/ps,ts->pt/dot_general | solution.py:57
  87.0 2.6 collective-permute-start.2
  89.7 78.0 %while.45 = (s32[]{:T(128)}, f32[8,5,512]{2,1,0:T(8,128)S(1)}, s32[4096,2]{0,1:T(2,128)S(1)}, s32[8]{0:T(128)S(1)}, f32[4096,2]{0,1:T(2,128)S(1)}, /*index=5*/f32[5,4096]{1,0:T(8,128)S(1)}, s32[]{:T(128)}) while((s32[]{:T(128)}, f32[8,5,512]{2,1,0:T(8,128)S(1)}, s32[4096,2]{0,1:T(2,128)S(1)}, s32[8]{0:T(128)S(1)}, f32[4096,2]{0,1:T(2,128)S(1)}, ...), condition=%wide.region_3.4_spmd, body=%wide.region_2.3_spmd.sunk | while | flops 136315392 | bytes 348265 | solution.py:60
  91.0 8.4 %fusion.148 = f32[8,5,512]{2,1,0:T(8,128)S(1)} fusion(f32[8,5,512]{2,1,0:T(8,128)S(1)} %get-tuple-element.470, s32[]{:T(128)S(6)} %copy.107, f32[5,4096]{1,0:T(8,128)S(1)} %get-tuple-element.481, f32[4096]{0:T(1024)S(1)} %bitcast.242, s32[4096]{0:T(1024)S(1)} %bitcast.250, f32[4096]{0:T(1024)S(1)} %bitcast.241, s32[4096]{0:T(1024)S(1)} %bitcast.249, ...), kind=kOutput, calls=%fused_computation.29.clone.1 | convolution fusion | flops 136314880 | bytes 215044 | tf_op jit(solution)/shard_map/while/body/eval_jaxpr/ps,ts->pt/dot_general | solution.py:57
  100.8 8.4 %fusion.148 = f32[8,5,512]{2,1,0:T(8,128)S(1)} fusion(f32[8,5,512]{2,1,0:T(8,128)S(1)} %get-tuple-element.470, s32[]{:T(128)S(6)} %copy.107, f32[5,4096]{1,0:T(8,128)S(1)} %get-tuple-element.481, f32[4096]{0:T(1024)S(1)} %bitcast.242, s32[4096]{0:T(1024)S(1)} %bitcast.250, f32[4096]{0:T(1024)S(1)} %bitcast.241, s32[4096]{0:T(1024)S(1)} %bitcast.249, ...), kind=kOutput, calls=%fused_computation.29.clone.1 | convolution fusion | flops 136314880 | bytes 215044 | tf_op jit(solution)/shard_map/while/body/eval_jaxpr/ps,ts->pt/dot_general | solution.py:57
  110.5 8.4 %fusion.148 = f32[8,5,512]{2,1,0:T(8,128)S(1)} fusion(f32[8,5,512]{2,1,0:T(8,128)S(1)} %get-tuple-element.470, s32[]{:T(128)S(6)} %copy.107, f32[5,4096]{1,0:T(8,128)S(1)} %get-tuple-element.481, f32[4096]{0:T(1024)S(1)} %bitcast.242, s32[4096]{0:T(1024)S(1)} %bitcast.250, f32[4096]{0:T(1024)S(1)} %bitcast.241, s32[4096]{0:T(1024)S(1)} %bitcast.249, ...), kind=kOutput, calls=%fused_computation.29.clone.1 | convolution fusion | flops 136314880 | bytes 215044 | tf_op jit(solution)/shard_map/while/body/eval_jaxpr/ps,ts->pt/dot_general | solution.py:57
  120.3 8.4 %fusion.148 = f32[8,5,512]{2,1,0:T(8,128)S(1)} fusion(f32[8,5,512]{2,1,0:T(8,128)S(1)} %get-tuple-element.470, s32[]{:T(128)S(6)} %copy.107, f32[5,4096]{1,0:T(8,128)S(1)} %get-tuple-element.481, f32[4096]{0:T(1024)S(1)} %bitcast.242, s32[4096]{0:T(1024)S(1)} %bitcast.250, f32[4096]{0:T(1024)S(1)} %bitcast.241, s32[4096]{0:T(1024)S(1)} %bitcast.249, ...), kind=kOutput, calls=%fused_computation.29.clone.1 | convolution fusion | flops 136314880 | bytes 215044 | tf_op jit(solution)/shard_map/while/body/eval_jaxpr/ps,ts->pt/dot_general | solution.py:57
  130.0 8.4 %fusion.148 = f32[8,5,512]{2,1,0:T(8,128)S(1)} fusion(f32[8,5,512]{2,1,0:T(8,128)S(1)} %get-tuple-element.470, s32[]{:T(128)S(6)} %copy.107, f32[5,4096]{1,0:T(8,128)S(1)} %get-tuple-element.481, f32[4096]{0:T(1024)S(1)} %bitcast.242, s32[4096]{0:T(1024)S(1)} %bitcast.250, f32[4096]{0:T(1024)S(1)} %bitcast.241, s32[4096]{0:T(1024)S(1)} %bitcast.249, ...), kind=kOutput, calls=%fused_computation.29.clone.1 | convolution fusion | flops 136314880 | bytes 215044 | tf_op jit(solution)/shard_map/while/body/eval_jaxpr/ps,ts->pt/dot_general | solution.py:57
  139.7 8.4 %fusion.148 = f32[8,5,512]{2,1,0:T(8,128)S(1)} fusion(f32[8,5,512]{2,1,0:T(8,128)S(1)} %get-tuple-element.470, s32[]{:T(128)S(6)} %copy.107, f32[5,4096]{1,0:T(8,128)S(1)} %get-tuple-element.481, f32[4096]{0:T(1024)S(1)} %bitcast.242, s32[4096]{0:T(1024)S(1)} %bitcast.250, f32[4096]{0:T(1024)S(1)} %bitcast.241, s32[4096]{0:T(1024)S(1)} %bitcast.249, ...), kind=kOutput, calls=%fused_computation.29.clone.1 | convolution fusion | flops 136314880 | bytes 215044 | tf_op jit(solution)/shard_map/while/body/eval_jaxpr/ps,ts->pt/dot_general | solution.py:57
  149.5 8.4 %fusion.148 = f32[8,5,512]{2,1,0:T(8,128)S(1)} fusion(f32[8,5,512]{2,1,0:T(8,128)S(1)} %get-tuple-element.470, s32[]{:T(128)S(6)} %copy.107, f32[5,4096]{1,0:T(8,128)S(1)} %get-tuple-element.481, f32[4096]{0:T(1024)S(1)} %bitcast.242, s32[4096]{0:T(1024)S(1)} %bitcast.250, f32[4096]{0:T(1024)S(1)} %bitcast.241, s32[4096]{0:T(1024)S(1)} %bitcast.249, ...), kind=kOutput, calls=%fused_computation.29.clone.1 | convolution fusion | flops 136314880 | bytes 215044 | tf_op jit(solution)/shard_map/while/body/eval_jaxpr/ps,ts->pt/dot_general | solution.py:57
  159.2 8.4 %fusion.148 = f32[8,5,512]{2,1,0:T(8,128)S(1)} fusion(f32[8,5,512]{2,1,0:T(8,128)S(1)} %get-tuple-element.470, s32[]{:T(128)S(6)} %copy.107, f32[5,4096]{1,0:T(8,128)S(1)} %get-tuple-element.481, f32[4096]{0:T(1024)S(1)} %bitcast.242, s32[4096]{0:T(1024)S(1)} %bitcast.250, f32[4096]{0:T(1024)S(1)} %bitcast.241, s32[4096]{0:T(1024)S(1)} %bitcast.249, ...), kind=kOutput, calls=%fused_computation.29.clone.1 | convolution fusion | flops 136314880 | bytes 215044 | tf_op jit(solution)/shard_map/while/body/eval_jaxpr/ps,ts->pt/dot_general | solution.py:57
  167.7 1.0 bitcast_select_fusion.2
  168.7 3.1 collective-permute-start.3
  171.8 0.8 compare_select_fusion
  172.7 2.1 fusion.78
  174.8 0.9 stack.8
  175.7 1.9 fusion.87
  177.6 0.9 fusion.102
  178.5 0.9 fusion.101
  179.4 1.2 fusion.80
  180.7 3.7 %fusion.77 = f32[4,16,256,6,5]{2,1,0,4,3:T(8,128)S(1)} fusion(f32[4,16,256,5]{2,1,0,3:T(8,128)S(1)} %fusion.98, bf16[6,5,5,4,16,256]{5,4,3,2,1,0:T(8,128)(2,1)} %param.29), kind=kLoop, calls=%fused_computation.67 | loop fusion | flops 6881280 | bytes 7208960
  184.6 0.9 slice_bitcast_fusion
  185.6 0.7 fusion.111
  186.2 0.9 fusion.79
  187.2 4.1 %collective-permute-start.5 = (f32[2,5,4,1,256]{4,3,1,2,0:T(1,128)}, f32[2,5,4,1,256]{4,3,1,2,0:T(1,128)}, u32[]{:S(2)}, u32[]{:S(2)}) collective-permute-start(f32[2,5,4,1,256]{4,3,1,2,0:T(1,128)} %get-tuple-element.250), channel_id=1, source_target_pairs={{0,1},{1,2},{2,3},{4,5},{5,6},{6,7},{8,9},{9,10},{10,11},{12,13},{... | collective-permute-start | bytes 122888 | tf_op jit(solution)/shard_map/ppermute | solution.py:18
  191.2 1.5 collective-permute-start.4
  192.8 78.6 %while.46 = (s32[]{:T(128)}, f32[8,5,512]{2,1,0:T(8,128)S(1)}, s32[4096,2]{0,1:T(2,128)S(1)}, s32[8]{0:T(128)S(1)}, f32[4096,2]{0,1:T(2,128)S(1)}, /*index=5*/f32[5,4096]{1,0:T(8,128)S(1)}, s32[]{:T(128)}) while((s32[]{:T(128)}, f32[8,5,512]{2,1,0:T(8,128)S(1)}, s32[4096,2]{0,1:T(2,128)S(1)}, s32[8]{0:T(128)S(1)}, f32[4096,2]{0,1:T(2,128)S(1)}, ...), condition=%wide.region_5.6_spmd, body=%wide.region_4.5_spmd.sunk | while | flops 136315392 | bytes 348265 | solution.py:60
  194.2 8.4 %fusion.153 = f32[8,5,512]{2,1,0:T(8,128)S(1)} fusion(f32[8,5,512]{2,1,0:T(8,128)S(1)} %get-tuple-element.491, s32[]{:T(128)S(6)} %copy.114, f32[5,4096]{1,0:T(8,128)S(1)} %get-tuple-element.502, f32[4096]{0:T(1024)S(1)} %bitcast.244, s32[4096]{0:T(1024)S(1)} %bitcast.252, f32[4096]{0:T(1024)S(1)} %bitcast.243, s32[4096]{0:T(1024)S(1)} %bitcast.251, ...), kind=kOutput, calls=%fused_computation.45.clone.1 | convolution fusion | flops 136314880 | bytes 215044 | tf_op jit(solution)/shard_map/while/body/eval_jaxpr/ps,ts->pt/dot_general | solution.py:57
  204.1 8.4 %fusion.153 = f32[8,5,512]{2,1,0:T(8,128)S(1)} fusion(f32[8,5,512]{2,1,0:T(8,128)S(1)} %get-tuple-element.491, s32[]{:T(128)S(6)} %copy.114, f32[5,4096]{1,0:T(8,128)S(1)} %get-tuple-element.502, f32[4096]{0:T(1024)S(1)} %bitcast.244, s32[4096]{0:T(1024)S(1)} %bitcast.252, f32[4096]{0:T(1024)S(1)} %bitcast.243, s32[4096]{0:T(1024)S(1)} %bitcast.251, ...), kind=kOutput, calls=%fused_computation.45.clone.1 | convolution fusion | flops 136314880 | bytes 215044 | tf_op jit(solution)/shard_map/while/body/eval_jaxpr/ps,ts->pt/dot_general | solution.py:57
  213.9 8.4 %fusion.153 = f32[8,5,512]{2,1,0:T(8,128)S(1)} fusion(f32[8,5,512]{2,1,0:T(8,128)S(1)} %get-tuple-element.491, s32[]{:T(128)S(6)} %copy.114, f32[5,4096]{1,0:T(8,128)S(1)} %get-tuple-element.502, f32[4096]{0:T(1024)S(1)} %bitcast.244, s32[4096]{0:T(1024)S(1)} %bitcast.252, f32[4096]{0:T(1024)S(1)} %bitcast.243, s32[4096]{0:T(1024)S(1)} %bitcast.251, ...), kind=kOutput, calls=%fused_computation.45.clone.1 | convolution fusion | flops 136314880 | bytes 215044 | tf_op jit(solution)/shard_map/while/body/eval_jaxpr/ps,ts->pt/dot_general | solution.py:57
  223.7 8.4 %fusion.153 = f32[8,5,512]{2,1,0:T(8,128)S(1)} fusion(f32[8,5,512]{2,1,0:T(8,128)S(1)} %get-tuple-element.491, s32[]{:T(128)S(6)} %copy.114, f32[5,4096]{1,0:T(8,128)S(1)} %get-tuple-element.502, f32[4096]{0:T(1024)S(1)} %bitcast.244, s32[4096]{0:T(1024)S(1)} %bitcast.252, f32[4096]{0:T(1024)S(1)} %bitcast.243, s32[4096]{0:T(1024)S(1)} %bitcast.251, ...), kind=kOutput, calls=%fused_computation.45.clone.1 | convolution fusion | flops 136314880 | bytes 215044 | tf_op jit(solution)/shard_map/while/body/eval_jaxpr/ps,ts->pt/dot_general | solution.py:57
  233.5 8.4 %fusion.153 = f32[8,5,512]{2,1,0:T(8,128)S(1)} fusion(f32[8,5,512]{2,1,0:T(8,128)S(1)} %get-tuple-element.491, s32[]{:T(128)S(6)} %copy.114, f32[5,4096]{1,0:T(8,128)S(1)} %get-tuple-element.502, f32[4096]{0:T(1024)S(1)} %bitcast.244, s32[4096]{0:T(1024)S(1)} %bitcast.252, f32[4096]{0:T(1024)S(1)} %bitcast.243, s32[4096]{0:T(1024)S(1)} %bitcast.251, ...), kind=kOutput, calls=%fused_computation.45.clone.1 | convolution fusion | flops 136314880 | bytes 215044 | tf_op jit(solution)/shard_map/while/body/eval_jaxpr/ps,ts->pt/dot_general | solution.py:57
  243.4 8.4 %fusion.153 = f32[8,5,512]{2,1,0:T(8,128)S(1)} fusion(f32[8,5,512]{2,1,0:T(8,128)S(1)} %get-tuple-element.491, s32[]{:T(128)S(6)} %copy.114, f32[5,4096]{1,0:T(8,128)S(1)} %get-tuple-element.502, f32[4096]{0:T(1024)S(1)} %bitcast.244, s32[4096]{0:T(1024)S(1)} %bitcast.252, f32[4096]{0:T(1024)S(1)} %bitcast.243, s32[4096]{0:T(1024)S(1)} %bitcast.251, ...), kind=kOutput, calls=%fused_computation.45.clone.1 | convolution fusion | flops 136314880 | bytes 215044 | tf_op jit(solution)/shard_map/while/body/eval_jaxpr/ps,ts->pt/dot_general | solution.py:57
  253.2 8.4 %fusion.153 = f32[8,5,512]{2,1,0:T(8,128)S(1)} fusion(f32[8,5,512]{2,1,0:T(8,128)S(1)} %get-tuple-element.491, s32[]{:T(128)S(6)} %copy.114, f32[5,4096]{1,0:T(8,128)S(1)} %get-tuple-element.502, f32[4096]{0:T(1024)S(1)} %bitcast.244, s32[4096]{0:T(1024)S(1)} %bitcast.252, f32[4096]{0:T(1024)S(1)} %bitcast.243, s32[4096]{0:T(1024)S(1)} %bitcast.251, ...), kind=kOutput, calls=%fused_computation.45.clone.1 | convolution fusion | flops 136314880 | bytes 215044 | tf_op jit(solution)/shard_map/while/body/eval_jaxpr/ps,ts->pt/dot_general | solution.py:57
  263.0 8.4 %fusion.153 = f32[8,5,512]{2,1,0:T(8,128)S(1)} fusion(f32[8,5,512]{2,1,0:T(8,128)S(1)} %get-tuple-element.491, s32[]{:T(128)S(6)} %copy.114, f32[5,4096]{1,0:T(8,128)S(1)} %get-tuple-element.502, f32[4096]{0:T(1024)S(1)} %bitcast.244, s32[4096]{0:T(1024)S(1)} %bitcast.252, f32[4096]{0:T(1024)S(1)} %bitcast.243, s32[4096]{0:T(1024)S(1)} %bitcast.251, ...), kind=kOutput, calls=%fused_computation.45.clone.1 | convolution fusion | flops 136314880 | bytes 215044 | tf_op jit(solution)/shard_map/while/body/eval_jaxpr/ps,ts->pt/dot_general | solution.py:57
  271.9 0.7 copy.77
  272.6 85.9 %while.47 = (s32[]{:T(128)}, f32[8,5,512]{2,1,0:T(8,128)S(1)}, s32[4096,2]{0,1:T(2,128)S(1)}, s32[8]{0:T(128)S(1)}, f32[4096,2]{0,1:T(2,128)S(1)}, /*index=5*/f32[5,4096]{1,0:T(8,128)}, s32[]{:T(128)}) while((s32[]{:T(128)}, f32[8,5,512]{2,1,0:T(8,128)S(1)}, s32[4096,2]{0,1:T(2,128)S(1)}, s32[8]{0:T(128)S(1)}, f32[4096,2]{0,1:T(2,128)S(1)}, ...), condition=%wide.region_7.8_spmd, body=%wide.region_6.7_spmd.sunk | while | flops 136315392 | bytes 299113 | solution.py:60
  273.4 0.7 iota_add_fusion.11
  274.0 9.3 %fusion.158 = f32[8,5,512]{2,1,0:T(8,128)S(1)} fusion(f32[8,5,512]{2,1,0:T(8,128)S(1)} %get-tuple-element.512, s32[]{:T(128)S(6)} %copy.121, f32[5,4096]{1,0:T(8,128)} %get-tuple-element.523, f32[4096]{0:T(1024)S(1)} %bitcast.246, s32[4096]{0:T(1024)S(1)} %bitcast.254, f32[4096]{0:T(1024)S(1)} %bitcast.245, s32[4096]{0:T(1024)S(1)} %bitcast.253, ...), kind=kOutput, calls=%fused_computation.61.clone.1 | convolution fusion | flops 136314880 | bytes 165892 | tf_op jit(solution)/shard_map/while/body/eval_jaxpr/ps,ts->pt/dot_general | solution.py:57
  284.8 9.3 %fusion.158 = f32[8,5,512]{2,1,0:T(8,128)S(1)} fusion(f32[8,5,512]{2,1,0:T(8,128)S(1)} %get-tuple-element.512, s32[]{:T(128)S(6)} %copy.121, f32[5,4096]{1,0:T(8,128)} %get-tuple-element.523, f32[4096]{0:T(1024)S(1)} %bitcast.246, s32[4096]{0:T(1024)S(1)} %bitcast.254, f32[4096]{0:T(1024)S(1)} %bitcast.245, s32[4096]{0:T(1024)S(1)} %bitcast.253, ...), kind=kOutput, calls=%fused_computation.61.clone.1 | convolution fusion | flops 136314880 | bytes 165892 | tf_op jit(solution)/shard_map/while/body/eval_jaxpr/ps,ts->pt/dot_general | solution.py:57
  295.5 9.3 %fusion.158 = f32[8,5,512]{2,1,0:T(8,128)S(1)} fusion(f32[8,5,512]{2,1,0:T(8,128)S(1)} %get-tuple-element.512, s32[]{:T(128)S(6)} %copy.121, f32[5,4096]{1,0:T(8,128)} %get-tuple-element.523, f32[4096]{0:T(1024)S(1)} %bitcast.246, s32[4096]{0:T(1024)S(1)} %bitcast.254, f32[4096]{0:T(1024)S(1)} %bitcast.245, s32[4096]{0:T(1024)S(1)} %bitcast.253, ...), kind=kOutput, calls=%fused_computation.61.clone.1 | convolution fusion | flops 136314880 | bytes 165892 | tf_op jit(solution)/shard_map/while/body/eval_jaxpr/ps,ts->pt/dot_general | solution.py:57
  306.2 9.3 %fusion.158 = f32[8,5,512]{2,1,0:T(8,128)S(1)} fusion(f32[8,5,512]{2,1,0:T(8,128)S(1)} %get-tuple-element.512, s32[]{:T(128)S(6)} %copy.121, f32[5,4096]{1,0:T(8,128)} %get-tuple-element.523, f32[4096]{0:T(1024)S(1)} %bitcast.246, s32[4096]{0:T(1024)S(1)} %bitcast.254, f32[4096]{0:T(1024)S(1)} %bitcast.245, s32[4096]{0:T(1024)S(1)} %bitcast.253, ...), kind=kOutput, calls=%fused_computation.61.clone.1 | convolution fusion | flops 136314880 | bytes 165892 | tf_op jit(solution)/shard_map/while/body/eval_jaxpr/ps,ts->pt/dot_general | solution.py:57
  317.0 9.3 %fusion.158 = f32[8,5,512]{2,1,0:T(8,128)S(1)} fusion(f32[8,5,512]{2,1,0:T(8,128)S(1)} %get-tuple-element.512, s32[]{:T(128)S(6)} %copy.121, f32[5,4096]{1,0:T(8,128)} %get-tuple-element.523, f32[4096]{0:T(1024)S(1)} %bitcast.246, s32[4096]{0:T(1024)S(1)} %bitcast.254, f32[4096]{0:T(1024)S(1)} %bitcast.245, s32[4096]{0:T(1024)S(1)} %bitcast.253, ...), kind=kOutput, calls=%fused_computation.61.clone.1 | convolution fusion | flops 136314880 | bytes 165892 | tf_op jit(solution)/shard_map/while/body/eval_jaxpr/ps,ts->pt/dot_general | solution.py:57
  327.7 9.3 %fusion.158 = f32[8,5,512]{2,1,0:T(8,128)S(1)} fusion(f32[8,5,512]{2,1,0:T(8,128)S(1)} %get-tuple-element.512, s32[]{:T(128)S(6)} %copy.121, f32[5,4096]{1,0:T(8,128)} %get-tuple-element.523, f32[4096]{0:T(1024)S(1)} %bitcast.246, s32[4096]{0:T(1024)S(1)} %bitcast.254, f32[4096]{0:T(1024)S(1)} %bitcast.245, s32[4096]{0:T(1024)S(1)} %bitcast.253, ...), kind=kOutput, calls=%fused_computation.61.clone.1 | convolution fusion | flops 136314880 | bytes 165892 | tf_op jit(solution)/shard_map/while/body/eval_jaxpr/ps,ts->pt/dot_general | solution.py:57
  338.4 9.3 %fusion.158 = f32[8,5,512]{2,1,0:T(8,128)S(1)} fusion(f32[8,5,512]{2,1,0:T(8,128)S(1)} %get-tuple-element.512, s32[]{:T(128)S(6)} %copy.121, f32[5,4096]{1,0:T(8,128)} %get-tuple-element.523, f32[4096]{0:T(1024)S(1)} %bitcast.246, s32[4096]{0:T(1024)S(1)} %bitcast.254, f32[4096]{0:T(1024)S(1)} %bitcast.245, s32[4096]{0:T(1024)S(1)} %bitcast.253, ...), kind=kOutput, calls=%fused_computation.61.clone.1 | convolution fusion | flops 136314880 | bytes 165892 | tf_op jit(solution)/shard_map/while/body/eval_jaxpr/ps,ts->pt/dot_general | solution.py:57
  348.5 0.7 iota_add_fusion.11
  349.2 9.3 %fusion.158 = f32[8,5,512]{2,1,0:T(8,128)S(1)} fusion(f32[8,5,512]{2,1,0:T(8,128)S(1)} %get-tuple-element.512, s32[]{:T(128)S(6)} %copy.121, f32[5,4096]{1,0:T(8,128)} %get-tuple-element.523, f32[4096]{0:T(1024)S(1)} %bitcast.246, s32[4096]{0:T(1024)S(1)} %bitcast.254, f32[4096]{0:T(1024)S(1)} %bitcast.245, s32[4096]{0:T(1024)S(1)} %bitcast.253, ...), kind=kOutput, calls=%fused_computation.61.clone.1 | convolution fusion | flops 136314880 | bytes 165892 | tf_op jit(solution)/shard_map/while/body/eval_jaxpr/ps,ts->pt/dot_general | solution.py:57
  358.6 4.8 %collective-permute-start.7 = (f32[5,16,256]{2,1,0:T(8,128)S(1)}, f32[5,16,256]{2,1,0:T(8,128)S(1)}, u32[]{:S(2)}, u32[]{:S(2)}) collective-permute-start(f32[5,16,256]{2,1,0:T(8,128)S(1)} %bitcast_select_fusion), channel_id=1, source_target_pairs={{0,28},{4,0},{8,4},{12,8},{16,12},{20,16},{24,20},{28,24},{1,29},{... | collective-permute-start | bytes 245768 | tf_op jit(solution)/shard_map/ppermute | solution.py:26
  363.4 1.4 fusion.93
  364.8 0.9 fusion.100
  366.0 0.8 bitcast_subtract_fusion
  (184 shorter events, 42.4 us)
Async XLA Ops:
  3.8 6.2 %copy-start.2 = (s32[16,256,2]{1,2,0:T(2,128)S(1)}, s32[16,256,2]{1,2,0:T(2,128)}, u32[]{:S(2)}) copy-start(s32[16,256,2]{1,2,0:T(2,128)} %param.33) | copy-start | bytes 98308
  3.8 6.2 %copy-start.3 = (f32[16,256,2]{1,2,0:T(2,128)S(1)}, f32[16,256,2]{1,2,0:T(2,128)}, u32[]{:S(2)}) copy-start(f32[16,256,2]{1,2,0:T(2,128)} %param.34) | copy-start | bytes 98308
  4.7 170.9 %collective-permute-start.1 = (f32[2,5,4,1,256]{4,3,1,2,0:T(1,128)}, f32[2,5,4,1,256]{4,3,1,2,0:T(1,128)}, u32[]{:S(2)}, u32[]{:S(2)}) collective-permute-start(f32[2,5,4,1,256]{4,3,1,2,0:T(1,128)} %get-tuple-element.256), channel_id=1, source_target_pairs={{0,1},{1,2},{2,3},{4,5},{5,6},{6,7},{8,9},{9,10},{10,11},{12,13},{... | collective-permute-start | bytes 122888 | tf_op jit(solution)/shard_map/ppermute | solution.py:18
  7.7 168.0 %collective-permute-start = (f32[2,5,4,1,256]{4,3,1,2,0:T(1,128)}, f32[2,5,4,1,256]{4,3,1,2,0:T(1,128)}, u32[]{:S(2)}, u32[]{:S(2)}) collective-permute-start(f32[2,5,4,1,256]{4,3,1,2,0:T(1,128)} %get-tuple-element.255), channel_id=1, source_target_pairs={{1,0},{2,1},{3,2},{5,4},{6,5},{7,6},{9,8},{10,9},{11,10},{13,12},{... | collective-permute-start | bytes 122888 | tf_op jit(solution)/shard_map/ppermute | solution.py:19
  9.9 77.0 %copy-start.7 = (f32[5,4,16,256]{3,2,0,1:T(8,128)}, f32[5,4,16,256]{3,2,0,1:T(8,128)S(1)}, u32[]{:S(2)}) copy-start(f32[5,4,16,256]{3,2,0,1:T(8,128)S(1)} %get-tuple-element.259) | copy-start | bytes 983044
  9.9 79.6 %copy-start.8 = (f32[5,4,16,256]{3,2,0,1:T(8,128)}, f32[5,4,16,256]{3,2,0,1:T(8,128)S(1)}, u32[]{:S(2)}) copy-start(f32[5,4,16,256]{3,2,0,1:T(8,128)S(1)} %get-tuple-element.260) | copy-start | bytes 983044
  10.0 79.6 %copy-start.4 = (s32[16,256,2]{1,2,0:T(2,128)S(1)}, s32[16,256,2]{1,2,0:T(2,128)}, u32[]{:S(2)}) copy-start(s32[16,256,2]{1,2,0:T(2,128)} %param.31) | copy-start | bytes 98308
  10.1 79.6 %copy-start.5 = (f32[16,256,2]{1,2,0:T(2,128)S(1)}, f32[16,256,2]{1,2,0:T(2,128)}, u32[]{:S(2)}) copy-start(f32[16,256,2]{1,2,0:T(2,128)} %param.32) | copy-start | bytes 98308
  87.0 90.6 %collective-permute-start.2 = (f32[5,16,256]{2,1,0:T(8,128)S(1)}, f32[5,16,256]{2,1,0:T(8,128)}, u32[]{:S(2)}, u32[]{:S(2)}) collective-permute-start(f32[5,16,256]{2,1,0:T(8,128)S(1)} %bitcast_select_fusion.3), channel_id=1, source_target_pairs={{0,4},{4,8},{8,12},{12,16},{16,20},{20,24},{24,28},{28,0},{1,5},{5... | collective-permute-start | bytes 245768 | tf_op jit(solution)/shard_map/ppermute | solution.py:26
  89.7 83.0 %copy-start = (f32[5,4,16,256]{3,2,1,0:T(8,128)S(1)}, f32[5,4,16,256]{3,2,1,0:T(8,128)}, u32[]{:S(2)}) copy-start(f32[5,4,16,256]{3,2,1,0:T(8,128)} %param.26) | copy-start | bytes 983044
  167.6 11.8 %copy-start.1 = (bf16[5,5,4,16,256]{4,3,2,1,0:T(8,128)(2,1)S(1)}, bf16[5,5,4,16,256]{4,3,2,1,0:T(8,128)(2,1)}, u32[]{:S(2)}) copy-start(bf16[5,5,4,16,256]{4,3,2,1,0:T(8,128)(2,1)} %param.30) | copy-start | bytes 2457604
  168.7 9.8 %collective-permute-start.3 = (f32[5,16,256]{2,1,0:T(8,128)S(1)}, f32[5,16,256]{2,1,0:T(8,128)}, u32[]{:S(2)}, u32[]{:S(2)}) collective-permute-start(f32[5,16,256]{2,1,0:T(8,128)S(1)} %bitcast_select_fusion.2), channel_id=1, source_target_pairs={{0,28},{4,0},{8,4},{12,8},{16,12},{20,16},{24,20},{28,24},{1,29},{... | collective-permute-start | bytes 245768 | tf_op jit(solution)/shard_map/ppermute | solution.py:26
  184.4 1.9 copy-start.6
  187.2 176.2 %collective-permute-start.5 = (f32[2,5,4,1,256]{4,3,1,2,0:T(1,128)}, f32[2,5,4,1,256]{4,3,1,2,0:T(1,128)}, u32[]{:S(2)}, u32[]{:S(2)}) collective-permute-start(f32[2,5,4,1,256]{4,3,1,2,0:T(1,128)} %get-tuple-element.250), channel_id=1, source_target_pairs={{0,1},{1,2},{2,3},{4,5},{5,6},{6,7},{8,9},{9,10},{10,11},{12,13},{... | collective-permute-start | bytes 122888 | tf_op jit(solution)/shard_map/ppermute | solution.py:18
  191.2 172.1 %collective-permute-start.4 = (f32[2,5,4,1,256]{4,3,1,2,0:T(1,128)}, f32[2,5,4,1,256]{4,3,1,2,0:T(1,128)}, u32[]{:S(2)}, u32[]{:S(2)}) collective-permute-start(f32[2,5,4,1,256]{4,3,1,2,0:T(1,128)} %get-tuple-element.249), channel_id=1, source_target_pairs={{1,0},{2,1},{3,2},{5,4},{6,5},{7,6},{9,8},{10,9},{11,10},{13,12},{... | collective-permute-start | bytes 122888 | tf_op jit(solution)/shard_map/ppermute | solution.py:19
  271.5 93.3 %collective-permute-start.6 = (f32[5,16,256]{2,1,0:T(8,128)S(1)}, f32[5,16,256]{2,1,0:T(8,128)}, u32[]{:S(2)}, u32[]{:S(2)}) collective-permute-start(f32[5,16,256]{2,1,0:T(8,128)S(1)} %bitcast_select_fusion.1), channel_id=1, source_target_pairs={{0,4},{4,8},{8,12},{12,16},{16,20},{20,24},{24,28},{28,0},{1,5},{5... | collective-permute-start | bytes 245768 | tf_op jit(solution)/shard_map/ppermute | solution.py:26
  272.6 93.2 %copy-start.9 = (f32[5,4,16,256]{3,2,1,0:T(8,128)S(1)}, f32[5,4,16,256]{3,2,1,0:T(8,128)}, u32[]{:S(2)}) copy-start(f32[5,4,16,256]{3,2,1,0:T(8,128)} %param.27) | copy-start | bytes 983044
  358.6 7.1 %collective-permute-start.7 = (f32[5,16,256]{2,1,0:T(8,128)S(1)}, f32[5,16,256]{2,1,0:T(8,128)S(1)}, u32[]{:S(2)}, u32[]{:S(2)}) collective-permute-start(f32[5,16,256]{2,1,0:T(8,128)S(1)} %bitcast_select_fusion), channel_id=1, source_target_pairs={{0,28},{4,0},{8,4},{12,8},{16,12},{20,16},{24,20},{28,24},{1,29},{... | collective-permute-start | bytes 245768 | tf_op jit(solution)/shard_map/ppermute | solution.py:26
where the time goes:
time: 369 us; the launch traced here: 367 us
  matrix products  276 us (75%)
  other arithmetic  40.9 us (11%)
  local copies, waits for them, and re-layouts  27.8 us (8%)
  starting transfers between devices  20.5 us (6%)
    dot_general x32, matrix products, one_block(): jnp.einsum('ps,ts->pt', flat_values, matrix, precision=lax.Precision.HIGH...  276 us
    add x32, other arithmetic, one_block(): targets = start + lax.iota(jnp.int32, width)  20.2 us
    dynamic_slice x32, local copies, waits for them, and re-layouts, scatter_face(): pieces = lax.map(one_block, starts)  19.8 us
    ppermute x4, starting transfers between devices, passed_along(): lax.ppermute(shard, axis, [(i, (i + by) % size) for i in range(size)])  10.7 us
    unnamed x5, other arithmetic  10.6 us
  transfers between devices with their start and end apart: 8, of which 0 were waited for; matrix products, arithmetic and copies ran while one was open for 90% of the time, Pallas kernels for 0%

commit v1 on v0

v1 whole, which is shorter than its diff:
```python
import functools

import jax
import jax.numpy as jnp
from jax import lax
from jax.experimental import pallas as pl
from jax.experimental.pallas import tpu as pltpu
from jax.sharding import PartitionSpec as P

ITERS = 2
MESH = pl.DeviceIdType.MESH
UNROLL = 4


def kernel(
    dims,
    adj_h, grad_h, diag_h, off_h, pre_h, ld_h, lw_h, hd_h, hw_h, tip_h,
    out,
    adj, grad, diag, off, pre, tabd, tabw, tip,
    onehot, face, scat, acc,
    s_up, s_dn, r_up, r_dn, s_left, s_right, r_left, r_right,
    load_sem, send_sem, recv_sem,
):
    pitches, spans, nv, lp, rows, nx, entries = dims
    top = lp - 1
    bits = nx.bit_length() - 1
    pi = lax.axis_index("pitch")
    si = lax.axis_index("span")
    above = lax.rem(pi + 1, pitches)
    below = lax.rem(pi + pitches - 1, pitches)
    is_first = pi == 0
    is_last = pi == pitches - 1
    is_end = jnp.logical_or(is_first, is_last)
    has_left = si > 0
    has_right = si < spans - 1

    barrier = pltpu.get_barrier_semaphore()
    pl.semaphore_signal(barrier, inc=1, device_id={"pitch": above}, device_id_type=MESH)
    pl.semaphore_signal(barrier, inc=1, device_id={"pitch": below}, device_id_type=MESH)

    @pl.when(has_left)
    def _():
        pl.semaphore_signal(barrier, inc=1, device_id={"span": si - 1}, device_id_type=MESH)

    @pl.when(has_right)
    def _():
        pl.semaphore_signal(barrier, inc=1, device_id={"span": si + 1}, device_id_type=MESH)

    def load(src, dst, n):
        return pltpu.make_async_copy(src, dst, load_sem.at[n])

    low_d, low_w = load(ld_h, tabd, 0), load(lw_h, tabw, 1)
    high_d, high_w = load(hd_h, tabd, 0), load(hw_h, tabw, 1)
    faces = [
        load(adj_h, adj, 2),
        load(off_h.at[0, :, :, 0], off.at[0, :, :, 0], 3),
        load(off_h.at[1, :, :, top], off.at[1, :, :, top], 4),
    ]
    span_part = [load(off_h.at[2], off.at[2], 5), load(off_h.at[3], off.at[3], 6)]
    rest_part = [
        load(diag_h, diag, 7),
        load(off_h.at[4], off.at[4], 8),
        load(off_h.at[5], off.at[5], 9),
        load(off_h.at[0, :, :, pl.ds(1, top)], off.at[0, :, :, pl.ds(1, top)], 10),
        load(off_h.at[1, :, :, pl.ds(0, top)], off.at[1, :, :, pl.ds(0, top)], 11),
    ]
    last_part = [load(grad_h, grad, 12), load(pre_h, pre, 13), load(tip_h, tip, 14)]

    @pl.when(is_first)
    def _():
        low_d.start()
        low_w.start()

    @pl.when(jnp.logical_and(is_last, jnp.logical_not(is_first)))
    def _():
        high_d.start()
        high_w.start()

    for copy in faces + span_part + rest_part + last_part:
        copy.start()

    @pl.when(jnp.logical_not(has_left))
    def _():
        r_left[...] = jnp.zeros_like(r_left)

    @pl.when(jnp.logical_not(has_right))
    def _():
        r_right[...] = jnp.zeros_like(r_right)

    @pl.when(is_end)
    def _():
        low_d.wait()
        low_w.wait()
        axial = lax.broadcasted_iota(jnp.int32, (nx, nx), 0)

        @pl.loop(0, rows)
        def _(k):
            donors = tabd[k] & (nx - 1)
            for e in range(entries):
                hit = axial == donors[e:e + 1]
                onehot[k * entries + e] = jnp.where(hit, 1.0, 0.0).astype(jnp.bfloat16)

    row_id = lax.broadcasted_iota(jnp.int32, (rows, nx), 0)
    lane_id = lax.broadcasted_iota(jnp.int32, (rows, nx), 1)

    def product(blocks, b, i):
        total = None
        for a in range(nv):
            term = blocks(a, b)[i].astype(jnp.float32) * adj[a, i]
            total = term if total is None else total + term
        return total

    def along(d):
        return lambda a, b: off.at[d, a, b]

    def scatter():
        scat[...] = jnp.zeros_like(scat)

        @pl.loop(0, rows // UNROLL)
        def _(step):
            total = None
            for u in range(UNROLL):
                k = step * UNROLL + u
                target_rows = tabd[k] >> bits
                weights = tabw[k]
                values = [face[p, pl.ds(k, 1), :] for p in range(nv)]
                for e in range(entries):
                    here = row_id == target_rows[e:e + 1]
                    parts = []
                    for p in range(nv):
                        full = values[p] * weights[e:e + 1]
                        high = full.astype(jnp.bfloat16).astype(jnp.float32)
                        for piece in (high, full - high):
                            parts.append(jnp.where(here, piece, 0.0).astype(jnp.bfloat16))
                    left = jnp.concatenate(parts, axis=0)
                    term = lax.dot_general(
                        left, onehot[k * entries + e], (((1,), (1,)), ((), ())),
                        preferred_element_type=jnp.float32,
                    )
                    total = term if total is None else total + term
            scat[...] += total

    def scattered(p):
        at = 2 * p * rows
        return scat[at:at + rows, :] + scat[at + rows:at + 2 * rows, :]

    for it in range(ITERS):
        first = it == 0
        target = out if it == ITERS - 1 else adj

        def remote(src, dst, n, where):
            return pltpu.make_async_remote_copy(
                src_ref=src.at[it], dst_ref=dst.at[it],
                send_sem=send_sem.at[it, n], recv_sem=recv_sem.at[it, n],
                device_id=where, device_id_type=MESH,
            )

        up = remote(s_up, r_up, 0, {"pitch": above})
        down = remote(s_dn, r_dn, 1, {"pitch": below})
        to_left = remote(s_left, r_right, 2, {"span": si - 1})
        to_right = remote(s_right, r_left, 3, {"span": si + 1})

        if first:
            for copy in faces:
                copy.wait()

        @pl.loop(0, nv)
        def _(b):
            low = product(along(0), b, 0)
            high = product(along(1), b, top)
            s_dn[it, b] = low
            s_up[it, b] = high
            face[b] = jnp.where(is_first, low, high)

        if first:
            pl.semaphore_wait(barrier, 2 + has_left.astype(jnp.int32) + has_right.astype(jnp.int32))

        @pl.when(jnp.logical_not(is_last))
        def _():
            up.start()

        @pl.when(jnp.logical_not(is_first))
        def _():
            down.start()

        @pl.when(is_end)
        def _():
            scatter()

            @pl.when(is_first)
            def _():
                for p in range(nv):
                    s_dn[it, p] = scattered(p)
                down.start()

            @pl.when(is_last)
            def _():
                for p in range(nv):
                    s_up[it, p] = scattered(p)
                up.start()

        if first:
            for copy in span_part:
                copy.wait()

        @pl.loop(0, nv)
        def _(b):
            for i in range(lp):
                left = product(along(2), b, i)
                right = product(along(3), b, i)
                s_left[it, b, i:i + 1, :] = left[0:1]
                s_right[it, b, i:i + 1, :] = right[rows - 1:rows]
                acc[b, i] = (
                    jnp.where(row_id < rows - 1, pltpu.roll(left, rows - 1, 0), 0.0)
                    + jnp.where(row_id > 0, pltpu.roll(right, 1, 0), 0.0)
                )

        @pl.when(has_left)
        def _():
            to_left.start()

        @pl.when(has_right)
        def _():
            to_right.start()

        if first:
            for copy in rest_part:
                copy.wait()

        @pl.loop(0, nv)
        def _(b):
            for i in range(lp):
                total = acc[b, i] + product(lambda a, c: diag.at[a, c], b, i)
                back = product(along(4), b, i)
                ahead = product(along(5), b, i)
                total = total + jnp.where(lane_id < nx - 1, pltpu.roll(back, nx - 1, 1), 0.0)
                total = total + jnp.where(lane_id > 0, pltpu.roll(ahead, 1, 1), 0.0)
                if i < top:
                    total = total + product(along(0), b, i + 1)
                if i > 0:
                    total = total + product(along(1), b, i - 1)
                acc[b, i] = total

        if first:
            for copy in last_part:
                copy.wait()

        @pl.when(has_right)
        def _():
            to_left_in = remote(s_left, r_right, 2, {"span": si + 1})
            to_left_in.wait_recv()

        @pl.when(has_left)
        def _():
            to_right_in = remote(s_right, r_left, 3, {"span": si - 1})
            to_right_in.wait_recv()

        def finish(i):
            step = jnp.where(tip[i] == 1, 0.3, 0.6)
            rest = []
            for b in range(nv):
                total = acc[b, i] + grad[b, i]
                total = total + jnp.where(row_id == rows - 1, r_right[it, b, i:i + 1, :], 0.0)
                total = total + jnp.where(row_id == 0, r_left[it, b, i:i + 1, :], 0.0)
                if i == 0:
                    total = total + r_up[it, b]
                if i == top:
                    total = total + r_dn[it, b]
                rest.append(total)
            for a in range(nv):
                total = None
                for b in range(nv):
                    term = pre[a, b, i].astype(jnp.float32) * rest[b]
                    total = term if total is None else total + term
                target[a, i] = adj[a, i] - step * total

        for i in range(1, top):
            finish(i)
        up.wait_recv()
        if top == 0:
            down.wait_recv()
        finish(0)
        if top > 0:
            down.wait_recv()
            finish(top)

        up.wait_send()
        down.wait_send()

        @pl.when(has_left)
        def _():
            to_left.wait_send()

        @pl.when(has_right)
        def _():
            to_right.wait_send()


def body(sizes, adjoint, gradient, diag_blocks, off_blocks, precond,
         low_donor, low_weight, high_donor, high_weight, tip_mask):
    pitches, spans = sizes
    nv, lp, rows, nx = adjoint.shape
    entries = low_donor.shape[2]
    dims = (pitches, spans, nv, lp, rows, nx, entries)
    tables = [jnp.swapaxes(t, 1, 2) for t in (low_donor, low_weight, high_donor, high_weight)]
    f32 = jnp.float32
    whole = pltpu.VMEM((nv, lp, rows, nx), f32)
    pitch_face = pltpu.VMEM((ITERS, nv, rows, nx), f32)
    span_face = pltpu.VMEM((ITERS, nv, lp, nx), f32)
    return pl.pallas_call(
        functools.partial(kernel, dims),
        out_shape=jax.ShapeDtypeStruct(adjoint.shape, f32),
        in_specs=[pl.BlockSpec(memory_space=pl.ANY)] * 10,
        out_specs=pl.BlockSpec(memory_space=pltpu.VMEM),
        scratch_shapes=[
            whole, whole,
            pltpu.VMEM(diag_blocks.shape, jnp.bfloat16),
            pltpu.VMEM(off_blocks.shape, jnp.bfloat16),
            pltpu.VMEM(precond.shape, jnp.bfloat16),
            pltpu.VMEM((rows, entries, nx), jnp.int32),
            pltpu.VMEM((rows, entries, nx), f32),
            pltpu.VMEM(tip_mask.shape, jnp.int32),
            pltpu.VMEM((rows * entries, nx, nx), jnp.bfloat16),
            pltpu.VMEM((nv, rows, nx), f32),
            pltpu.VMEM((2 * nv * rows, nx), f32),
            whole,
            pitch_face, pitch_face, pitch_face, pitch_face,
            span_face, span_face, span_face, span_face,
            pltpu.SemaphoreType.DMA((15,)),
            pltpu.SemaphoreType.DMA((ITERS, 4)),
            pltpu.SemaphoreType.DMA((ITERS, 4)),
        ],
        compiler_params=pltpu.CompilerParams(
            collective_id=0, has_side_effects=True, vmem_limit_bytes=56 * 1024 * 1024
        ),
    )(adjoint, gradient, diag_blocks, off_blocks, precond, *tables, tip_mask)


def solution(mesh):
    sizes = (mesh.shape["pitch"], mesh.shape["span"])
    return jax.shard_map(
        functools.partial(body, sizes),
        mesh=mesh,
        in_specs=(
            P(None, "pitch", "span", None),
            P(None, "pitch", "span", None),
            P(None, None, "pitch", "span", None),
            P(None, None, None, "pitch", "span", None),
            P(None, None, "pitch", "span", None),
            P("span", None, None),
            P("span", None, None),
            P("span", None, None),
            P("span", None, None),
            P("pitch", "span", None),
        ),
        out_specs=P(None, "pitch", "span", None),
        check_vma=False,
    )
```

time: 369 us -> 22.8 us (0.06)
  matrix products: 276 us -> 0 us
  other arithmetic: 40.9 us -> 0 us
  local copies, waits for them, and re-layouts: 27.8 us -> 1.72 us
  Pallas kernels: 0 us -> 20.9 us
  starting transfers between devices: 20.5 us -> 0 us
    dot_general x32 -> x0, matrix products: 276 us -> none  [one_block(): jnp.einsum('ps,ts->pt', flat_values, matrix, precision=lax.Precision.HIGH...]
    add x34 -> x0, other arithmetic: 23.6 us -> none  [the longest x32 20.2 us: one_block(): targets = start + lax.iota(jnp.int32, width)]
    pallas_call x0 -> x1, Pallas kernels: none -> 20.9 us  [body(): pl.pallas_call(functools.partial(kernel, dims), out_shape=jax.ShapeDtypeS...]
    ppermute x8 -> x0, starting transfers between devices: 20.5 us -> none  [the longest x4 10.7 us: passed_along(): lax.ppermute(shard, axis, [(i, (i + by) % size) for i in range(size)])]
    dynamic_slice x32 -> x0, local copies, waits for them, and re-layouts: 19.8 us -> none  [scatter_face(): pieces = lax.map(one_block, starts)]
    unnamed x5 -> x0, other arithmetic: 10.6 us -> none
  transfers between devices with their start and end apart: 8 -> 0, of which waited for: 0 -> 0; matrix products, arithmetic and copies ran while one was open for 90% -> 0% of each run, Pallas kernels for 0% -> 0%
where the time goes in v1:
time: 22.8 us; the launch traced here: 22.6 us
  Pallas kernels  20.9 us (92%)
  local copies, waits for them, and re-layouts  1.72 us (8%)
    pallas_call x1, Pallas kernels, body(): pl.pallas_call(functools.partial(kernel, dims), out_shape=jax.ShapeDtypeS...  20.9 us
    unnamed x1, local copies, waits for them, and re-layouts  1.72 us

profile of v1, /device:TPU:0, one launch (start us, length us, event | category | flops | bytes accessed | tf_op | source)
XLA Modules:
  0.0 22.6 jit_solution(9153505661421811497)
XLA Ops:
  0.0 20.9 %shard_map.100 = f32[5,4,16,256]{3,2,1,0:T(8,128)} custom-call(f32[5,4,16,256]{3,2,1,0:T(8,128)} %adj_h.1, f32[5,4,16,256]{3,2,1,0:T(8,128)} %grad_h.1, bf16[5,5,4,16,256]{4,3,2,1,0:T(8,128)(2,1)} %diag_h.1, bf16[6,5,5,4,16,256]{5,4,3,2,1,0:T(8,128)(2,1)} %off_h.1, bf16[5,5,4,16,256]{4,3,2,1,0:T(8,128)(2,1)} %pre_h.1, s32[16,2,256]{2,1,0:T(2,128)} %bitcast.4, ...), custom_call_target="tpu_custom_call" | custom-call | tf_op jit(solution)/shard_map/pallas_call | solution.py:310
  20.9 1.7 %copy.12 = f32[5,4,16,256]{3,2,1,0:T(8,128)} copy(f32[5,4,16,256]{3,2,1,0:T(8,128)} %shard_map.100) | data formatting | bytes 655360

commit v2 on v1

--- a/solution.py
+++ b/solution.py
@@ -10,6 +10,7 @@
 ITERS = 2
 MESH = pl.DeviceIdType.MESH
 UNROLL = 4
+CHUNKS = 2
 
 
 def kernel(
@@ -17,7 +18,7 @@
     adj_h, grad_h, diag_h, off_h, pre_h, ld_h, lw_h, hd_h, hw_h, tip_h,
     out,
     adj, grad, diag, off, pre, tabd, tabw, tip,
-    onehot, face, scat, acc,
+    onehot, in_row, tab2, pieces, scat, acc,
     s_up, s_dn, r_up, r_dn, s_left, s_right, r_left, r_right,
     load_sem, send_sem, recv_sem,
 ):
@@ -66,12 +67,12 @@
     ]
     last_part = [load(grad_h, grad, 12), load(pre_h, pre, 13), load(tip_h, tip, 14)]
 
-    @pl.when(is_first)
+    @pl.when(is_last)
     def _():
         low_d.start()
         low_w.start()
 
-    @pl.when(jnp.logical_and(is_last, jnp.logical_not(is_first)))
+    @pl.when(jnp.logical_and(is_first, jnp.logical_not(is_last)))
     def _():
         high_d.start()
         high_w.start()
@@ -93,12 +94,18 @@
         low_w.wait()
         axial = lax.broadcasted_iota(jnp.int32, (nx, nx), 0)
 
+        span_row = lax.broadcasted_iota(jnp.int32, (rows, nx), 0)
+
         @pl.loop(0, rows)
         def _(k):
-            donors = tabd[k] & (nx - 1)
+            donors = tabd[k]
+            weights = tabw[k]
             for e in range(entries):
-                hit = axial == donors[e:e + 1]
+                hit = axial == donors[e:e + 1] & (nx - 1)
                 onehot[k * entries + e] = jnp.where(hit, 1.0, 0.0).astype(jnp.bfloat16)
+                here = span_row == donors[e:e + 1] >> bits
+                in_row[k * entries + e] = jnp.where(here, 1.0, 0.0).astype(jnp.bfloat16)
+                tab2[e, pl.ds(k, 1), :] = weights[e:e + 1]
 
     row_id = lax.broadcasted_iota(jnp.int32, (rows, nx), 0)
     lane_id = lax.broadcasted_iota(jnp.int32, (rows, nx), 1)
@@ -113,36 +120,43 @@
     def along(d):
         return lambda a, b: off.at[d, a, b]
 
-    def scatter():
-        scat[...] = jnp.zeros_like(scat)
-
-        @pl.loop(0, rows // UNROLL)
+    def scatter(it, c):
+        part = rows // CHUNKS
+        here = pl.ds(c * part, part)
+        for p in range(nv):
+            value = jnp.where(is_first, r_up[it, p, here, :], r_dn[it, p, here, :])
+            for e in range(entries):
+                full = value * tab2[e, here, :]
+                high = full.astype(jnp.bfloat16).astype(jnp.float32)
+                pieces[e, 2 * p, here, :] = high
+                pieces[e, 2 * p + 1, here, :] = full - high
+
+        @pl.loop(0, part // UNROLL)
         def _(step):
             total = None
             for u in range(UNROLL):
-                k = step * UNROLL + u
-                target_rows = tabd[k] >> bits
-                weights = tabw[k]
-                values = [face[p, pl.ds(k, 1), :] for p in range(nv)]
+                k = c * part + step * UNROLL + u
                 for e in range(entries):
-                    here = row_id == target_rows[e:e + 1]
+                    mask = in_row[k * entries + e]
                     parts = []
-                    for p in range(nv):
-                        full = values[p] * weights[e:e + 1]
-                        high = full.astype(jnp.bfloat16).astype(jnp.float32)
-                        for piece in (high, full - high):
-                            parts.append(jnp.where(here, piece, 0.0).astype(jnp.bfloat16))
-                    left = jnp.concatenate(parts, axis=0)
+                    for q in range(2 * nv):
+                        row = jnp.broadcast_to(pieces[e, q, pl.ds(k, 1), :], (rows, nx))
+                        parts.append(row.astype(jnp.bfloat16) * mask)
                     term = lax.dot_general(
-                        left, onehot[k * entries + e], (((1,), (1,)), ((), ())),
-                        preferred_element_type=jnp.float32,
+                        jnp.concatenate(parts, axis=0), onehot[k * entries + e],
+                        (((1,), (1,)), ((), ())), preferred_element_type=jnp.float32,
                     )
                     total = term if total is None else total + term
-            scat[...] += total
+            scat[c] = total if part == UNROLL else scat[c] + total
 
     def scattered(p):
         at = 2 * p * rows
-        return scat[at:at + rows, :] + scat[at + rows:at + 2 * rows, :]
+        total = None
+        for c in range(CHUNKS):
+            for start in (at, at + rows):
+                term = scat[c, start:start + rows, :]
+                total = term if total is None else total + term
+        return total
 
     for it in range(ITERS):
         first = it == 0
@@ -155,8 +169,16 @@
                 device_id=where, device_id_type=MESH,
             )
 
-        up = remote(s_up, r_up, 0, {"pitch": above})
-        down = remote(s_dn, r_dn, 1, {"pitch": below})
+        def remote_part(src, dst, n, c, where):
+            here = pl.ds(c * (rows // CHUNKS), rows // CHUNKS)
+            return pltpu.make_async_remote_copy(
+                src_ref=src.at[it, :, here], dst_ref=dst.at[it, :, here],
+                send_sem=send_sem.at[it, n + c], recv_sem=recv_sem.at[it, n + c],
+                device_id=where, device_id_type=MESH,
+            )
+
+        up = [remote_part(s_up, r_up, 4, c, {"pitch": above}) for c in range(CHUNKS)]
+        down = [remote_part(s_dn, r_dn, 4 + CHUNKS, c, {"pitch": below}) for c in range(CHUNKS)]
         to_left = remote(s_left, r_right, 2, {"span": si - 1})
         to_right = remote(s_right, r_left, 3, {"span": si + 1})
 
@@ -170,34 +192,13 @@
             high = product(along(1), b, top)
             s_dn[it, b] = low
             s_up[it, b] = high
-            face[b] = jnp.where(is_first, low, high)
 
         if first:
             pl.semaphore_wait(barrier, 2 + has_left.astype(jnp.int32) + has_right.astype(jnp.int32))
 
-        @pl.when(jnp.logical_not(is_last))
-        def _():
-            up.start()
-
-        @pl.when(jnp.logical_not(is_first))
-        def _():
-            down.start()
-
-        @pl.when(is_end)
-        def _():
-            scatter()
-
-            @pl.when(is_first)
-            def _():
-                for p in range(nv):
-                    s_dn[it, p] = scattered(p)
-                down.start()
-
-            @pl.when(is_last)
-            def _():
-                for p in range(nv):
-                    s_up[it, p] = scattered(p)
-                up.start()
+        for c in range(CHUNKS):
+            up[c].start()
+            down[c].start()
 
         if first:
             for copy in span_part:
@@ -276,16 +277,38 @@
 
         for i in range(1, top):
             finish(i)
-        up.wait_recv()
-        if top == 0:
-            down.wait_recv()
+        @pl.when(is_end)
+        def _():
+            if rows // CHUNKS != UNROLL:
+                scat[...] = jnp.zeros_like(scat)
+            for c in range(CHUNKS):
+                up[c].wait_recv()
+                down[c].wait_recv()
+                scatter(it, c)
+
+            @pl.when(is_first)
+            def _():
+                for p in range(nv):
+                    r_up[it, p] = scattered(p)
+
+            @pl.when(is_last)
+            def _():
+                for p in range(nv):
+                    r_dn[it, p] = scattered(p)
+
+        @pl.when(jnp.logical_not(is_end))
+        def _():
+            for c in range(CHUNKS):
+                up[c].wait_recv()
+                down[c].wait_recv()
+
         finish(0)
         if top > 0:
-            down.wait_recv()
             finish(top)
 
-        up.wait_send()
-        down.wait_send()
+        for c in range(CHUNKS):
+            up[c].wait_send()
+            down[c].wait_send()
 
         @pl.when(has_left)
         def _():
@@ -309,7 +332,7 @@
     span_face = pltpu.VMEM((ITERS, nv, lp, nx), f32)
     return pl.pallas_call(
         functools.partial(kernel, dims),
-        out_shape=jax.ShapeDtypeStruct(adjoint.shape, f32),
+        out_shape=pltpu.VMEM(adjoint.shape, f32),
         in_specs=[pl.BlockSpec(memory_space=pl.ANY)] * 10,
         out_specs=pl.BlockSpec(memory_space=pltpu.VMEM),
         scratch_shapes=[
@@ -321,14 +344,16 @@
             pltpu.VMEM((rows, entries, nx), f32),
             pltpu.VMEM(tip_mask.shape, jnp.int32),
             pltpu.VMEM((rows * entries, nx, nx), jnp.bfloat16),
-            pltpu.VMEM((nv, rows, nx), f32),
-            pltpu.VMEM((2 * nv * rows, nx), f32),
+            pltpu.VMEM((rows * entries, rows, nx), jnp.bfloat16),
+            pltpu.VMEM((entries, rows, nx), f32),
+            pltpu.VMEM((entries, 2 * nv, rows, nx), f32),
+            pltpu.VMEM((CHUNKS, 2 * nv * rows, nx), f32),
             whole,
             pitch_face, pitch_face, pitch_face, pitch_face,
             span_face, span_face, span_face, span_face,
             pltpu.SemaphoreType.DMA((15,)),
-            pltpu.SemaphoreType.DMA((ITERS, 4)),
-            pltpu.SemaphoreType.DMA((ITERS, 4)),
+            pltpu.SemaphoreType.DMA((ITERS, 4 + 2 * CHUNKS)),
+            pltpu.SemaphoreType.DMA((ITERS, 4 + 2 * CHUNKS)),
         ],
         compiler_params=pltpu.CompilerParams(
             collective_id=0, has_side_effects=True, vmem_limit_bytes=56 * 1024 * 1024

time: 22.8 us -> 20.4 us (0.89)
  Pallas kernels: 20.9 us -> 19.5 us
  local copies, waits for them, and re-layouts: 1.72 us -> 0.73 us
    pallas_call x1, Pallas kernels: 20.9 us -> 19.5 us  [body(): pl.pallas_call(functools.partial(kernel, dims), out_shape=pltpu.VMEM(adjo...]
    unnamed x1, local copies, waits for them, and re-layouts: 1.72 us -> 0.73 us
where the time goes in v2:
time: 20.4 us; the launch traced here: 20.2 us
  Pallas kernels  19.5 us (96%)
  local copies, waits for them, and re-layouts  0.73 us (4%)
    pallas_call x1, Pallas kernels, body(): pl.pallas_call(functools.partial(kernel, dims), out_shape=pltpu.VMEM(adjo...  19.5 us
    unnamed x1, local copies, waits for them, and re-layouts  0.73 us

profile of v2, /device:TPU:0, one launch (start us, length us, event | category | flops | bytes accessed | tf_op | source)
XLA Modules:
  0.0 20.2 jit_solution(6596766758163800621)
XLA Ops:
  0.0 19.5 %shard_map.100 = f32[5,4,16,256]{3,2,1,0:T(8,128)S(1)} custom-call(f32[5,4,16,256]{3,2,1,0:T(8,128)} %adj_h.1, f32[5,4,16,256]{3,2,1,0:T(8,128)} %grad_h.1, bf16[5,5,4,16,256]{4,3,2,1,0:T(8,128)(2,1)} %diag_h.1, bf16[6,5,5,4,16,256]{5,4,3,2,1,0:T(8,128)(2,1)} %off_h.1, bf16[5,5,4,16,256]{4,3,2,1,0:T(8,128)(2,1)} %pre_h.1, s32[16,2,256]{2,1,0:T(2,128)} %bitcast.4, ...), custom_call_target="tpu_custom_call" | custom-call | tf_op jit(solution)/shard_map/pallas_call | solution.py:333
  19.5 0.7 %copy.12 = f32[5,4,16,256]{3,2,1,0:T(8,128)} copy(f32[5,4,16,256]{3,2,1,0:T(8,128)S(1)} %shard_map.100) | data formatting | bytes 655360

commit v3 on v2

--- a/solution.py
+++ b/solution.py
@@ -9,8 +9,8 @@
 
 ITERS = 2
 MESH = pl.DeviceIdType.MESH
-UNROLL = 4
-CHUNKS = 2
+UNROLL = 16
+CHUNKS = 1
 
 
 def kernel(
@@ -102,7 +102,7 @@
             weights = tabw[k]
             for e in range(entries):
                 hit = axial == donors[e:e + 1] & (nx - 1)
-                onehot[k * entries + e] = jnp.where(hit, 1.0, 0.0).astype(jnp.bfloat16)
+                onehot[k * entries + e] = jnp.where(hit, 1.0, 0.0).T.astype(jnp.bfloat16)
                 here = span_row == donors[e:e + 1] >> bits
                 in_row[k * entries + e] = jnp.where(here, 1.0, 0.0).astype(jnp.bfloat16)
                 tab2[e, pl.ds(k, 1), :] = weights[e:e + 1]
@@ -144,7 +144,7 @@
                         parts.append(row.astype(jnp.bfloat16) * mask)
                     term = lax.dot_general(
                         jnp.concatenate(parts, axis=0), onehot[k * entries + e],
-                        (((1,), (1,)), ((), ())), preferred_element_type=jnp.float32,
+                        (((1,), (0,)), ((), ())), preferred_element_type=jnp.float32,
                     )
                     total = term if total is None else total + term
             scat[c] = total if part == UNROLL else scat[c] + total
@@ -196,9 +196,21 @@
         if first:
             pl.semaphore_wait(barrier, 2 + has_left.astype(jnp.int32) + has_right.astype(jnp.int32))
 
-        for c in range(CHUNKS):
-            up[c].start()
-            down[c].start()
+        @pl.when(is_first)
+        def _():
+            for c in range(CHUNKS):
+                down[c].start()
+
+        @pl.when(jnp.logical_not(is_first))
+        def _():
+            for c in range(CHUNKS):
+                up[c].start()
+
+        @pl.when(jnp.logical_not(is_end))
+        def _():
+            for c in range(CHUNKS):
+                down[c].start()
+
 
         if first:
             for copy in span_part:
@@ -241,6 +253,16 @@
                 if i > 0:
                     total = total + product(along(1), b, i - 1)
                 acc[b, i] = total
+
+        @pl.when(is_first)
+        def _():
+            for c in range(CHUNKS):
+                up[c].start()
+
+        @pl.when(is_last)
+        def _():
+            for c in range(CHUNKS):
+                down[c].start()
 
         if first:
             for copy in last_part:

time: 20.4 us -> 19 us (0.931)
  Pallas kernels: 19.5 us -> 18.2 us
    pallas_call x1, Pallas kernels: 19.5 us -> 18.2 us  [body(): pl.pallas_call(functools.partial(kernel, dims), out_shape=pltpu.VMEM(adjo...]
where the time goes in v3:
time: 19 us; the launch traced here: 18.9 us
  Pallas kernels  18.2 us (96%)
  local copies, waits for them, and re-layouts  0.73 us (4%)
    pallas_call x1, Pallas kernels, body(): pl.pallas_call(functools.partial(kernel, dims), out_shape=pltpu.VMEM(adjo...  18.2 us
    unnamed x1, local copies, waits for them, and re-layouts  0.73 us

profile of v3, /device:TPU:0, one launch (start us, length us, event | category | flops | bytes accessed | tf_op | source)
XLA Modules:
  0.0 18.9 jit_solution(4414331841976229270)
XLA Ops:
  0.0 18.2 %shard_map.100 = f32[5,4,16,256]{3,2,1,0:T(8,128)S(1)} custom-call(f32[5,4,16,256]{3,2,1,0:T(8,128)} %adj_h.1, f32[5,4,16,256]{3,2,1,0:T(8,128)} %grad_h.1, bf16[5,5,4,16,256]{4,3,2,1,0:T(8,128)(2,1)} %diag_h.1, bf16[6,5,5,4,16,256]{5,4,3,2,1,0:T(8,128)(2,1)} %off_h.1, bf16[5,5,4,16,256]{4,3,2,1,0:T(8,128)(2,1)} %pre_h.1, s32[16,2,256]{2,1,0:T(2,128)} %bitcast.4, ...), custom_call_target="tpu_custom_call" | custom-call | tf_op jit(solution)/shard_map/pallas_call | solution.py:355
  18.2 0.7 %copy.12 = f32[5,4,16,256]{3,2,1,0:T(8,128)} copy(f32[5,4,16,256]{3,2,1,0:T(8,128)S(1)} %shard_map.100) | data formatting | bytes 655360
